TPU v7x, 32 devices: a whole 2x2x4 slice. The times are simulated.
32 devices in a mesh: ex: 8 (over z, x), tp: 4 (over y, core).
Axes of the slice: x: 2, y: 2, z: 4, core: 2. Of those that a mesh axis runs over, the one named last changes fastest.
Arguments:
- activations: bfloat16 [32, 128, 8192], P('ex', None, 'tp'), may hold values from -6 to 6
- out_grads: bfloat16 [32, 128, 8192], P('ex', None, 'tp'), may hold values from -0.5390625 to 0.5390625
Outputs:
- fisher: float32 [8192, 8192], P('ex', 'tp')
All inputs are finite; a program needn't handle non-finite values.
Results may differ from a plain program's by a relative error of at most 0.0003.
Values may be sent and summed in bfloat16 or wider, within the bound.
A program may use at most 128 MiB of HBM per device.

v0:
```python
import math

import jax
import jax.numpy as jnp
from jax import lax
from jax.sharding import PartitionSpec as P


def body(activations, out_grads):
    width_out = out_grads.shape[2]
    width_local = activations.shape[2]
    full_width = width_local * lax.axis_size("tp")
    own_rows = full_width // lax.axis_size("ex")
    whole_inputs = lax.all_gather(activations, "tp", axis=2, tiled=True)
    block_rows = math.gcd(lax.axis_size("ex") * own_rows, 512)

    def one_block(position, result):
        window = lax.dynamic_slice_in_dim(whole_inputs, position * block_rows, block_rows, 2)
        gradient = jnp.einsum("etd,etc->edc", window, out_grads, preferred_element_type=jnp.float32)
        squared = jnp.sum(gradient * gradient, axis=0)
        return lax.dynamic_update_slice_in_dim(result, squared, position * block_rows, 0)

    initial = jnp.zeros((lax.axis_size("ex") * own_rows, width_out), jnp.float32)
    return lax.psum_scatter(
        lax.fori_loop(0, lax.axis_size("ex") * own_rows // block_rows, one_block, initial),
        "ex",
        scatter_dimension=0,
        tiled=True,
    )


def solution(mesh):
    return jax.shard_map(
        body,
        mesh=mesh,
        in_specs=(P("ex", None, "tp"), P("ex", None, "tp")),
        out_specs=P("ex", "tp"),
        check_vma=False,
    )
```

profile of v0, /device:TPU:0, one launch (start us, length us, event | category | flops | bytes accessed | tf_op | source)
XLA Modules:
  0.0 1254.2 jit_solution(10314185727028201062)
XLA Ops:
  6.5 3.9 copy.3
  10.6 61.1 %all-gather.2.cloned.1.call-done = bf16[4,128,8192]{1,2,0:T(8,128)(2,1)} async-done(((bf16[4,128,2048]{1,2,0:T(8,128)(2,1)}), bf16[4,128,8192]{1,2,0:T(8,128)(2,1)}) %all-gather.2.cloned.1.call-update) | async-done | bytes 8388624 | tf_op jit(solution)/shard_map/all_gather | solution.py:14
  71.6 21.2 %broadcast_in_dim.3 = f32[8192,2048]{1,0:T(8,128)} broadcast(f32[]{:T(128)} %constant.37.clone.1), dimensions={} | broadcast | bytes 67108864 | tf_op jit(solution)/shard_map/broadcast_in_dim | solution.py:23
  92.9 98.1 %while.13 = (s32[]{:T(128)}, f32[8192,2048]{1,0:T(8,128)}, bf16[4,128,8192]{1,2,0:T(8,128)(2,1)}, bf16[4,128,2048]{2,1,0:T(8,128)(2,1)S(1)}, s32[]{:T(128)}, /*index=5*/s32[]{:T(128)}, s32[]{:T(128)}, s32[]{:T(128)}) while((s32[]{:T(128)}, f32[8192,2048]{1,0:T(8,128)}, bf16[4,128,8192]{1,2,0:T(8,128)(2,1)}, ...), condition=%wide.region_2.0_spmd, body=%wide.region_0.0_spmd.sunk | while | flops 1081081856 | bytes 15204491 | solution.py:25
  92.9 3.7 multiply_reduce_fusion.2
  99.0 3.7 multiply_reduce_fusion.2
  102.6 2.5 constant_dynamic-update-slice_fusion.2
  105.1 3.7 multiply_reduce_fusion.2
  111.3 3.7 multiply_reduce_fusion.2
  117.4 3.7 multiply_reduce_fusion.2
  123.5 3.7 multiply_reduce_fusion.2
  129.6 3.7 multiply_reduce_fusion.2
  135.7 3.7 multiply_reduce_fusion.2
  141.9 3.7 multiply_reduce_fusion.2
  145.5 2.6 constant_dynamic-update-slice_fusion.2
  148.1 3.7 multiply_reduce_fusion.2
  154.2 3.7 multiply_reduce_fusion.2
  160.3 3.7 multiply_reduce_fusion.2
  166.4 3.7 multiply_reduce_fusion.2
  170.1 2.5 constant_dynamic-update-slice_fusion.2
  172.6 3.7 multiply_reduce_fusion.2
  178.7 3.7 multiply_reduce_fusion.2
  184.8 3.7 multiply_reduce_fusion.2
  191.0 1056.4 %reduce-scatter.2.cloned.1.call-done = f32[1024,2048]{1,0:T(8,128)} async-done(((f32[8192,2048]{1,0:T(8,128)}), f32[1024,2048]{1,0:T(8,128)}) %reduce-scatter.2.cloned.1.call-update) | async-done | bytes 8388624 | tf_op jit(solution)/shard_map/reduce_scatter | solution.py:24
  (19 shorter events, 31.9 us)
Async XLA Ops:
  6.5 65.1 %all-gather.2.cloned.1.call-start = ((), (), s32[]{:S(2)}) async-start(), calls=%async_computation.1 | async-start | bytes 10485760 | tf_op jit(solution)/shard_map/all_gather | solution.py:14
  10.5 1236.9 %reduce-scatter.2.cloned.1.call-start = ((), (), s32[]{:S(2)}) async-start(), calls=%async_computation.2 | async-start | bytes 75497472 | tf_op jit(solution)/shard_map/reduce_scatter | solution.py:24
  10.5 82.3 %copy-start = (bf16[4,128,2048]{2,1,0:T(8,128)(2,1)S(1)}, bf16[4,128,2048]{2,1,0:T(8,128)(2,1)}, u32[]{:S(2)}) copy-start(bf16[4,128,2048]{2,1,0:T(8,128)(2,1)} %param.5) | copy-start | bytes 6291460
Sparse Core Ops, SparseCore 0:
  10.6 60.9 all-gather.1
  191.1 1056.2 reduce-scatter.1
where the time goes:
time: 1260 us; the launch traced here: 1250 us
  waiting for transfers between devices  1120 us (89%)
  local copies, waits for them, and re-layouts  64.6 us (5%)
  matrix products  58.6 us (5%)
  between operations  13.4 us (1%)
    reduce_scatter x1, waiting for transfers between devices, body(): lax.psum_scatter(lax.fori_loop(0, lax.axis_size('ex') * own_rows // block...  1060 us
    all_gather x1, waiting for transfers between devices, body(): whole_inputs = lax.all_gather(activations, 'tp', axis=2, tiled=True)  61.1 us
    dot_general x16, matrix products, one_block(): jnp.einsum('etd,etc->edc', window, out_grads, preferred_element_type=jnp....  58.6 us
    dynamic_update_slice x16, local copies, waits for them, and re-layouts, one_block(): lax.dynamic_update_slice_in_dim(result, squared, position * block_rows, 0)  39.4 us
  transfers between devices with their start and end apart: 2, of which 2 were waited for; matrix products, arithmetic and copies ran while one was open for 0% of the time, Pallas kernels for 0%

commit v1 on v0

v1 whole, which is shorter than its diff:
```python
import functools

import jax
import jax.numpy as jnp
from jax import lax
from jax.experimental import pallas as pl
from jax.experimental.pallas import tpu as pltpu
from jax.sharding import PartitionSpec as P

MESH = pl.DeviceIdType.MESH
LINE = 4
BY_LINE = 1
CORES = 2


def tile_of(size, most):
    while size % most:
        most //= 2
    return most


def kernel(n_ex, n_tp, act_ref, og_ref, out_ref, acts, ogs, acc, lhs,
           own_sem, og_recv, up_send, down_send, across_send,
           part_send, part_recv, y_send, sib_send, share_recv, out_sem):
    examples, tokens, width = og_ref.shape
    rows = acc.shape[0]
    line, wide = LINE, n_ex // LINE
    per_owner = width // rows
    ys = n_tp // CORES
    quarter = act_ref.shape[0] // n_tp

    me, tp = lax.axis_index("ex"), lax.axis_index("tp")
    z, x = me // wide, lax.rem(me, wide)
    y, core = tp // CORES, lax.rem(tp, CORES)
    owner = me // per_owner
    mine = owner == tp

    def chunk(zz, xx, k):
        return (zz * wide + xx) * examples + k

    def other(first, step, size):
        return lax.rem(first + step, size)

    barrier = pltpu.get_barrier_semaphore()

    def greet(ex, t):
        pl.semaphore_signal(barrier, inc=1, device_id={"ex": ex, "tp": t}, device_id_type=MESH)

    @pl.when(z > 0)
    def _():
        greet(me - wide, tp)

    @pl.when(z < line - 1)
    def _():
        greet(me + wide, tp)

    for d in range(1, wide):
        greet(z * wide + other(x, d, wide), tp)
    for d in range(1, ys):
        greet(me, other(y, d, ys) * CORES + core)
    greet(me, y * CORES + 1 - core)

    @pl.loop(0, n_ex)
    def _(ex):
        @pl.when(jnp.logical_not(jnp.logical_and(ex == me, mine)))
        def _():
            greet(ex, owner)

    count = (z > 0).astype(jnp.int32) + (z < line - 1).astype(jnp.int32) - mine.astype(jnp.int32)
    pl.semaphore_wait(barrier, count + (wide - 1) + (ys - 1) + 1 + per_owner * n_tp)

    def part(j, t):
        return pltpu.make_async_remote_copy(
            src_ref=act_ref.at[pl.ds(t * quarter, quarter), pl.ds(j * rows, rows)],
            dst_ref=acts.at[me, pl.ds(t * quarter, quarter)],
            send_sem=part_send.at[j * n_tp + t], recv_sem=part_recv.at[me],
            device_id={"ex": tp * per_owner + j, "tp": t}, device_id_type=MESH)

    def own_part(j):
        return pltpu.make_async_copy(
            act_ref.at[pl.ds(tp * quarter, quarter), pl.ds(j * rows, rows)],
            acts.at[me, pl.ds(tp * quarter, quarter)], part_recv.at[me])

    def piece(ex, t):
        return acts.at[ex, pl.ds(t * quarter, quarter)]

    def share_y(ex, d):
        return pltpu.make_async_remote_copy(
            src_ref=piece(ex, tp), dst_ref=piece(ex, tp),
            send_sem=y_send.at[ex * ys + d], recv_sem=share_recv.at[ex * n_tp + tp],
            device_id={"ex": me, "tp": other(y, d, ys) * CORES + core}, device_id_type=MESH)

    def share_core(ex, yy):
        t = yy * CORES + core
        return pltpu.make_async_remote_copy(
            src_ref=piece(ex, t), dst_ref=piece(ex, t),
            send_sem=sib_send.at[ex * ys + yy], recv_sem=share_recv.at[ex * n_tp + t],
            device_id={"ex": me, "tp": y * CORES + 1 - core}, device_id_type=MESH)

    def arrived(ref, sem):
        pltpu.make_async_copy(ref, ref, sem).wait()

    def og_copy(c, source, sems, slot, ex):
        return pltpu.make_async_remote_copy(
            src_ref=source, dst_ref=ogs.at[c], send_sem=sems.at[slot], recv_sem=og_recv.at[c],
            device_id={"ex": ex, "tp": tp}, device_id_type=MESH)

    def up(c, source):
        return og_copy(c, source, up_send, c, me + wide)

    def down(c, source):
        return og_copy(c, source, down_send, c, me - wide)

    def across(c, source, d):
        return og_copy(c, source, across_send, c * wide + d, z * wide + other(x, d, wide))

    def own_load():
        return pltpu.make_async_copy(og_ref, ogs.at[pl.ds(me * examples, examples)], own_sem)

    def each_part(act):
        @pl.loop(0, per_owner * n_tp)
        def _(i):
            j, t = i // n_tp, lax.rem(i, n_tp)
            itself = jnp.logical_and(tp * per_owner + j == me, t == tp)
            act(j, t, itself)

    def start_part(j, t, itself):
        @pl.when(itself)
        def _():
            own_part(j).start()

        @pl.when(jnp.logical_not(itself))
        def _():
            part(j, t).start()

    def end_part(j, t, itself):
        @pl.when(jnp.logical_not(itself))
        def _():
            part(j, t).wait_send()

    def own_copies(go):
        @pl.loop(0, examples)
        def _(k):
            c = chunk(z, x, k)
            for d in range(1, wide):
                go(across(c, og_ref.at[k], d))

            @pl.when(z < line - 1)
            def _():
                go(up(c, og_ref.at[k]))

            @pl.when(z > 0)
            def _():
                go(down(c, og_ref.at[k]))

    def line_copies(go, ready, s):
        @pl.loop(0, examples)
        def _(k):
            for step in (-1, 1):
                zz = z + step * s

                @pl.when(jnp.logical_and(zz >= 0, zz < line))
                def _():
                    c = chunk(zz, x, k)
                    ready(c)
                    if step < 0:
                        @pl.when(z < line - 1)
                        def _():
                            go(up(c, ogs.at[c]))
                    else:
                        @pl.when(z > 0)
                        def _():
                            go(down(c, ogs.at[c]))

                    @pl.when(jnp.logical_or(s > 1, k >= BY_LINE))
                    def _():
                        for d in range(1, wide):
                            go(across(c, ogs.at[c], d))

    def side_copies(go, ready):
        for k in range(BY_LINE):
            for d in range(1, wide):
                c = chunk(z, other(x, d, wide), k)
                ready(c)

                @pl.when(z < line - 1)
                def _():
                    go(up(c, ogs.at[c]))

                @pl.when(z > 0)
                def _():
                    go(down(c, ogs.at[c]))

    def start(copy):
        copy.start()

    def sent(copy):
        copy.wait_send()

    def og_ready(c):
        arrived(ogs.at[c], og_recv.at[c])

    def nothing(c):
        pass

    def act_parts(first, last):
        @pl.loop(first, last)
        def _(i):
            ex = lax.rem(me + i, n_ex)
            arrived(piece(ex, tp), part_recv.at[ex])
            for d in range(1, ys):
                share_y(ex, d).start()
            share_core(ex, y).start()

    def act_shares():
        @pl.loop(0, n_ex)
        def _(i):
            ex = lax.rem(me + i, n_ex)
            for d in range(1, ys):
                yy = other(y, d, ys)
                t = yy * CORES + core
                arrived(piece(ex, t), share_recv.at[ex * n_tp + t])
                share_core(ex, yy).start()

    each_part(start_part)
    own_copies(start)
    own_load().start()
    acc[...] = jnp.zeros_like(acc)
    line_copies(start, og_ready, 1)
    side_copies(start, og_ready)
    act_parts(0, n_ex // 2)
    for s in range(2, line):
        line_copies(start, og_ready, s)
        if s == 2:
            act_parts(n_ex // 2, n_ex)
    act_shares()
    own_load().wait()

    row_tile, col_tile = tile_of(rows, 256), tile_of(width, 512)

    def add_source(ex):
        @pl.loop(0, rows // row_tile)
        def _(i):
            r = pl.ds(pl.multiple_of(i * row_tile, row_tile), row_tile)
            for k in range(examples):
                lhs[k] = acts[ex, pl.ds(k * tokens, tokens), r].T

            @pl.loop(0, width // col_tile)
            def _(j):
                q = pl.ds(pl.multiple_of(j * col_tile, col_tile), col_tile)
                total = acc[r, q]
                for k in range(examples):
                    g = jnp.dot(lhs[k], ogs[ex * examples + k, :, q], preferred_element_type=jnp.float32)
                    total = total + g * g
                acc[r, q] = total

    spread = 2 * line - 1

    @pl.loop(0, wide * spread)
    def _(i):
        d, v = i // spread, lax.rem(i, spread)
        zz = z + ((v + 1) // 2) * (2 * lax.rem(v, 2) - 1)

        @pl.when(jnp.logical_and(zz >= 0, zz < line))
        def _():
            xx = other(x, d, wide)
            ex = zz * wide + xx
            for yy in range(ys):
                t = yy * CORES + 1 - core
                arrived(piece(ex, t), share_recv.at[ex * n_tp + t])

            @pl.when(d > 0)
            def _():
                @pl.loop(0, examples)
                def _(k):
                    @pl.when(jnp.logical_or(zz != z, k >= BY_LINE))
                    def _():
                        og_ready(chunk(zz, xx, k))

            add_source(ex)

    result = pltpu.make_async_copy(acc, out_ref, out_sem)
    result.start()

    each_part(end_part)
    own_copies(sent)
    for s in range(1, line):
        line_copies(sent, nothing, s)
    side_copies(sent, nothing)

    @pl.loop(0, n_ex)
    def _(ex):
        for d in range(1, ys):
            share_y(ex, d).wait_send()
        for yy in range(ys):
            share_core(ex, yy).wait_send()

    result.wait()


def solution(mesh):
    n_ex, n_tp = mesh.shape["ex"], mesh.shape["tp"]

    def body(activations, out_grads):
        examples, tokens, width = out_grads.shape
        rows = width * n_tp // n_ex
        flat = activations.reshape(examples * tokens, width)
        chunks = n_ex * examples
        wide = n_ex // LINE
        ys = n_tp // CORES
        dma = pltpu.SemaphoreType.DMA
        return pl.pallas_call(
            functools.partial(kernel, n_ex, n_tp),
            out_shape=jax.ShapeDtypeStruct((rows, width), jnp.float32),
            in_specs=[pl.BlockSpec(memory_space=pl.ANY)] * 2,
            out_specs=pl.BlockSpec(memory_space=pl.ANY),
            scratch_shapes=[
                pltpu.VMEM((n_ex, examples * tokens, rows), jnp.bfloat16),
                pltpu.VMEM((chunks, tokens, width), jnp.bfloat16),
                pltpu.VMEM((rows, width), jnp.float32),
                pltpu.VMEM((examples, tile_of(rows, 256), tokens), jnp.bfloat16),
                dma,
                dma((chunks,)),
                dma((chunks,)),
                dma((chunks,)),
                dma((chunks * wide,)),
                dma((width // rows * n_tp,)),
                dma((n_ex,)),
                dma((n_ex * ys,)),
                dma((n_ex * ys,)),
                dma((n_ex * n_tp,)),
                dma,
            ],
            compiler_params=pltpu.CompilerParams(
                collective_id=0, has_side_effects=True, vmem_limit_bytes=48 * 1024 * 1024),
            cost_estimate=pl.CostEstimate(
                flops=2 * rows * width * chunks * tokens,
                bytes_accessed=12 * 1024 * 1024, transcendentals=0),
        )(flat, out_grads)

    return jax.shard_map(
        body,
        mesh=mesh,
        in_specs=(P("ex", None, "tp"), P("ex", None, "tp")),
        out_specs=P("ex", "tp"),
        check_vma=False,
    )
```

time: 1260 us -> 301 us (0.24)
  waiting for transfers between devices: 1120 us -> 0 us
  Pallas kernels: 0 us -> 285 us
  matrix products: 58.6 us -> 0 us
  local copies, waits for them, and re-layouts: 64.6 us -> 11.1 us
  between operations: 13.4 us -> 0.01 us
    reduce_scatter x1 -> x0, waiting for transfers between devices: 1060 us -> none  [body(): lax.psum_scatter(lax.fori_loop(0, lax.axis_size('ex') * own_rows // block...]
    pallas_call x0 -> x1, Pallas kernels: none -> 285 us  [body(): pl.pallas_call(functools.partial(kernel, n_ex, n_tp), out_shape=jax.Shape...]
    all_gather x1 -> x0, waiting for transfers between devices: 61.1 us -> none  [body(): whole_inputs = lax.all_gather(activations, 'tp', axis=2, tiled=True)]
    dot_general x16 -> x0, matrix products: 58.6 us -> none  [one_block(): jnp.einsum('etd,etc->edc', window, out_grads, preferred_element_type=jnp....]
    dynamic_update_slice x16 -> x0, local copies, waits for them, and re-layouts: 39.4 us -> none  [one_block(): lax.dynamic_update_slice_in_dim(result, squared, position * block_rows, 0)]
    broadcast_in_dim x1 -> x0, local copies, waits for them, and re-layouts: 21.2 us -> none  [body(): jnp.zeros((lax.axis_size('ex') * own_rows, width_out), jnp.float32)]
  transfers between devices with their start and end apart: 2 -> 0, of which waited for: 2 -> 0; matrix products, arithmetic and copies ran while one was open for 0% -> 0% of each run, Pallas kernels for 0% -> 0%
where the time goes in v1:
time: 301 us; the launch traced here: 296 us
  Pallas kernels  285 us (95%)
  local copies, waits for them, and re-layouts  11.1 us (4%)
    pallas_call x1, Pallas kernels, body(): pl.pallas_call(functools.partial(kernel, n_ex, n_tp), out_shape=jax.Shape...  285 us
    unnamed x5, local copies, waits for them, and re-layouts  11.1 us

profile of v1, /device:TPU:0, one launch (start us, length us, event | category | flops | bytes accessed | tf_op | source)
XLA Modules:
  0.0 296.3 jit_solution(15048328084173375844)
XLA Ops:
  0.0 0.0 copy-start
  0.0 1.6 copy-done
  1.6 0.0 copy-start.1
  1.6 1.6 copy-done.1
  3.2 285.2 %shard_map.28 = f32[1024,2048]{1,0:T(8,128)} custom-call(bf16[512,2048]{1,0:T(8,128)(2,1)S(1)} %bitcast.1, bf16[4,128,2048]{2,1,0:T(8,128)(2,1)S(1)} %copy-done.1), custom_call_target="tpu_custom_call" | custom-call | flops 17179869184 | bytes 12582912 | tf_op jit(solution)/shard_map/pallas_call | solution.py:312
  288.4 7.9 %copy.4 = f32[1024,2048]{1,0:T(8,128)} copy(f32[1024,2048]{1,0:T(8,128)} %shard_map.28) | data formatting | bytes 16777216
Async XLA Ops:
  0.0 1.6 copy-start
  1.6 1.6 copy-start.1

commit v2 on v1

--- a/solution.py
+++ b/solution.py
@@ -19,11 +19,11 @@
     return most
 
 
-def kernel(n_ex, n_tp, act_ref, og_ref, out_ref, acts, ogs, acc, lhs,
+def kernel(n_ex, n_tp, act_ref, og_ref, out_ref, acts, ogs, lhs,
            own_sem, og_recv, up_send, down_send, across_send,
-           part_send, part_recv, y_send, sib_send, share_recv, out_sem):
+           part_send, part_recv, y_send, sib_send, share_recv):
     examples, tokens, width = og_ref.shape
-    rows = acc.shape[0]
+    rows = out_ref.shape[0]
     line, wide = LINE, n_ex // LINE
     per_owner = width // rows
     ys = n_tp // CORES
@@ -153,29 +153,27 @@
             def _():
                 go(down(c, og_ref.at[k]))
 
-    def line_copies(go, ready, s):
-        @pl.loop(0, examples)
-        def _(k):
-            for step in (-1, 1):
-                zz = z + step * s
-
-                @pl.when(jnp.logical_and(zz >= 0, zz < line))
+    def line_step(go, ready, s, k):
+        for step in (-1, 1):
+            zz = z + step * s
+
+            @pl.when(jnp.logical_and(zz >= 0, zz < line))
+            def _():
+                c = chunk(zz, x, k)
+                ready(c)
+                if step < 0:
+                    @pl.when(z < line - 1)
+                    def _():
+                        go(up(c, ogs.at[c]))
+                else:
+                    @pl.when(z > 0)
+                    def _():
+                        go(down(c, ogs.at[c]))
+
+                @pl.when(jnp.logical_or(s > 1, k >= BY_LINE))
                 def _():
-                    c = chunk(zz, x, k)
-                    ready(c)
-                    if step < 0:
-                        @pl.when(z < line - 1)
-                        def _():
-                            go(up(c, ogs.at[c]))
-                    else:
-                        @pl.when(z > 0)
-                        def _():
-                            go(down(c, ogs.at[c]))
-
-                    @pl.when(jnp.logical_or(s > 1, k >= BY_LINE))
-                    def _():
-                        for d in range(1, wide):
-                            go(across(c, ogs.at[c], d))
+                    for d in range(1, wide):
+                        go(across(c, ogs.at[c], d))
 
     def side_copies(go, ready):
         for k in range(BY_LINE):
@@ -203,89 +201,110 @@
     def nothing(c):
         pass
 
+    def act_source(i):
+        far = i // wide
+        below = jnp.minimum(z, line - 1 - z)
+        near = jnp.where(lax.rem(far, 2) == 1, z - (far + 1) // 2, z + far // 2)
+        end = jnp.where(z < line - 1 - z, far, line - 1 - far)
+        zz = jnp.where(far <= 2 * below, near, end)
+        return zz * wide + lax.rem(x + lax.rem(i, wide), wide)
+
     def act_parts(first, last):
         @pl.loop(first, last)
         def _(i):
-            ex = lax.rem(me + i, n_ex)
+            ex = act_source(i)
             arrived(piece(ex, tp), part_recv.at[ex])
             for d in range(1, ys):
                 share_y(ex, d).start()
             share_core(ex, y).start()
 
-    def act_shares():
-        @pl.loop(0, n_ex)
+    def act_shares(first, last):
+        @pl.loop(first, last)
         def _(i):
-            ex = lax.rem(me + i, n_ex)
+            ex = act_source(i)
             for d in range(1, ys):
                 yy = other(y, d, ys)
                 t = yy * CORES + core
                 arrived(piece(ex, t), share_recv.at[ex * n_tp + t])
                 share_core(ex, yy).start()
 
-    each_part(start_part)
-    own_copies(start)
-    own_load().start()
-    acc[...] = jnp.zeros_like(acc)
-    line_copies(start, og_ready, 1)
-    side_copies(start, og_ready)
-    act_parts(0, n_ex // 2)
-    for s in range(2, line):
-        line_copies(start, og_ready, s)
-        if s == 2:
-            act_parts(n_ex // 2, n_ex)
-    act_shares()
-    own_load().wait()
-
-    row_tile, col_tile = tile_of(rows, 256), tile_of(width, 512)
-
-    def add_source(ex):
-        @pl.loop(0, rows // row_tile)
-        def _(i):
-            r = pl.ds(pl.multiple_of(i * row_tile, row_tile), row_tile)
-            for k in range(examples):
-                lhs[k] = acts[ex, pl.ds(k * tokens, tokens), r].T
-
-            @pl.loop(0, width // col_tile)
-            def _(j):
-                q = pl.ds(pl.multiple_of(j * col_tile, col_tile), col_tile)
-                total = acc[r, q]
-                for k in range(examples):
-                    g = jnp.dot(lhs[k], ogs[ex * examples + k, :, q], preferred_element_type=jnp.float32)
-                    total = total + g * g
-                acc[r, q] = total
-
-    spread = 2 * line - 1
-
-    @pl.loop(0, wide * spread)
-    def _(i):
-        d, v = i // spread, lax.rem(i, spread)
-        zz = z + ((v + 1) // 2) * (2 * lax.rem(v, 2) - 1)
+    col_tile = tile_of(width, 512)
+
+    def add_example(ex, k):
+        lhs[...] = acts[ex, pl.ds(pl.multiple_of(k * tokens, tokens), tokens), :].T
+
+        @pl.loop(0, width // col_tile)
+        def _(j):
+            q = pl.ds(pl.multiple_of(j * col_tile, col_tile), col_tile)
+            g = jnp.dot(lhs[...], ogs[ex * examples + k, :, q], preferred_element_type=jnp.float32)
+            out_ref[:, q] += g * g
+
+    slots = wide + (line - 1) * 2 * wide
+
+    def add_source(n):
+        far = n >= wide
+        m = jnp.maximum(n - wide, 0)
+        s = jnp.where(far, 1 + m // (2 * wide), 0)
+        d = jnp.where(far, lax.rem(m, 2 * wide) // 2, n)
+        zz = z + s * (2 * lax.rem(m, 2) - 1)
 
         @pl.when(jnp.logical_and(zz >= 0, zz < line))
         def _():
-            xx = other(x, d, wide)
+            xx = lax.rem(x + d, wide)
             ex = zz * wide + xx
             for yy in range(ys):
                 t = yy * CORES + 1 - core
                 arrived(piece(ex, t), share_recv.at[ex * n_tp + t])
 
-            @pl.when(d > 0)
+            @pl.loop(0, examples)
+            def _(k):
+                @pl.when(jnp.logical_and(d > 0, jnp.logical_or(zz != z, k >= BY_LINE)))
+                def _():
+                    og_ready(chunk(zz, xx, k))
+
+                add_example(ex, k)
+
+    each_part(start_part)
+    own_copies(start)
+    own_load().start()
+    out_ref[...] = jnp.zeros_like(out_ref)
+    own_load().wait()
+    each = -(-n_ex // examples)
+    more = -(-n_ex // (2 * examples))
+
+    @pl.loop(0, examples + slots)
+    def _(i):
+        s, k = 1 + i // examples, lax.rem(i, examples)
+
+        @pl.when(s < line)
+        def _():
+            line_step(start, og_ready, s, k)
+
+        @pl.when(s == 1)
+        def _():
+            act_parts(k * each, jnp.minimum(k * each + each, n_ex))
+
+        @pl.when(i == examples - 1)
+        def _():
+            side_copies(start, og_ready)
+            act_shares(0, more)
+
+        @pl.when(i >= examples)
+        def _():
+            @pl.when(s == 2)
             def _():
-                @pl.loop(0, examples)
-                def _(k):
-                    @pl.when(jnp.logical_or(zz != z, k >= BY_LINE))
-                    def _():
-                        og_ready(chunk(zz, xx, k))
-
-            add_source(ex)
-
-    result = pltpu.make_async_copy(acc, out_ref, out_sem)
-    result.start()
+                first = more + k * each
+                act_shares(jnp.minimum(first, n_ex), jnp.minimum(first + each, n_ex))
+
+            add_source(i - examples)
 
     each_part(end_part)
     own_copies(sent)
-    for s in range(1, line):
-        line_copies(sent, nothing, s)
+
+    @pl.loop(0, (line - 1) * examples)
+    def _(i):
+        line_step(sent, nothing, 1 + i // examples, lax.rem(i, examples))
+
     side_copies(sent, nothing)
 
     @pl.loop(0, n_ex)
@@ -294,8 +313,6 @@
             share_y(ex, d).wait_send()
         for yy in range(ys):
             share_core(ex, yy).wait_send()
-
-    result.wait()
 
 
 def solution(mesh):
@@ -313,12 +330,11 @@
             functools.partial(kernel, n_ex, n_tp),
             out_shape=jax.ShapeDtypeStruct((rows, width), jnp.float32),
             in_specs=[pl.BlockSpec(memory_space=pl.ANY)] * 2,
-            out_specs=pl.BlockSpec(memory_space=pl.ANY),
+            out_specs=pl.BlockSpec(memory_space=pltpu.VMEM),
             scratch_shapes=[
                 pltpu.VMEM((n_ex, examples * tokens, rows), jnp.bfloat16),
                 pltpu.VMEM((chunks, tokens, width), jnp.bfloat16),
-                pltpu.VMEM((rows, width), jnp.float32),
-                pltpu.VMEM((examples, tile_of(rows, 256), tokens), jnp.bfloat16),
+                pltpu.VMEM((rows, tokens), jnp.bfloat16),
                 dma,
                 dma((chunks,)),
                 dma((chunks,)),
@@ -329,10 +345,9 @@
                 dma((n_ex * ys,)),
                 dma((n_ex * ys,)),
                 dma((n_ex * n_tp,)),
-                dma,
             ],
             compiler_params=pltpu.CompilerParams(
-                collective_id=0, has_side_effects=True, vmem_limit_bytes=48 * 1024 * 1024),
+                collective_id=0, has_side_effects=True, vmem_limit_bytes=40 * 1024 * 1024),
             cost_estimate=pl.CostEstimate(
                 flops=2 * rows * width * chunks * tokens,
                 bytes_accessed=12 * 1024 * 1024, transcendentals=0),

time: 301 us -> 260 us (0.86); the launches traced: 296 us -> 260 us
  Pallas kernels: 285 us -> 253 us
  local copies, waits for them, and re-layouts: 11.1 us -> 6.58 us
    pallas_call x1, Pallas kernels: 285 us -> 253 us  [body(): pl.pallas_call(functools.partial(kernel, n_ex, n_tp), out_shape=jax.Shape...]
    unnamed x5, local copies, waits for them, and re-layouts: 11.1 us -> 6.58 us
where the time goes in v2:
time: 260 us
  Pallas kernels  253 us (97%)
  local copies, waits for them, and re-layouts  6.58 us (3%)
    pallas_call x1, Pallas kernels, body(): pl.pallas_call(functools.partial(kernel, n_ex, n_tp), out_shape=jax.Shape...  253 us
    unnamed x5, local copies, waits for them, and re-layouts  6.58 us

profile of v2, /device:TPU:0, one launch (start us, length us, event | category | flops | bytes accessed | tf_op | source)
XLA Modules:
  0.0 259.7 jit_solution(18373519225813700770)
XLA Ops:
  0.0 0.0 copy-start
  0.0 1.6 copy-done
  1.6 0.0 copy-start.1
  1.6 1.6 copy-done.1
  3.2 253.1 %shard_map.28 = f32[1024,2048]{1,0:T(8,128)S(1)} custom-call(bf16[512,2048]{1,0:T(8,128)(2,1)S(1)} %bitcast.1, bf16[4,128,2048]{2,1,0:T(8,128)(2,1)S(1)} %copy-done.1), custom_call_target="tpu_custom_call" | custom-call | flops 17179869184 | bytes 12582912 | tf_op jit(solution)/shard_map/pallas_call | solution.py:329
  256.3 3.4 %copy.4 = f32[1024,2048]{1,0:T(8,128)} copy(f32[1024,2048]{1,0:T(8,128)S(1)} %shard_map.28) | data formatting | bytes 16777216
Async XLA Ops:
  0.0 1.6 copy-start
  1.6 1.6 copy-start.1

commit v3 on v2

--- a/solution.py
+++ b/solution.py
@@ -19,9 +19,9 @@
     return most
 
 
-def kernel(n_ex, n_tp, act_ref, og_ref, out_ref, acts, ogs, lhs,
+def kernel(n_ex, n_tp, act_ref, og_ref, out_ref, acts, ogs, relay, lhs,
            own_sem, og_recv, up_send, down_send, across_send,
-           part_send, part_recv, y_send, sib_send, share_recv):
+           part_send, part_recv, relay_send, relay_recv, y_send, sib_send, share_recv):
     examples, tokens, width = og_ref.shape
     rows = out_ref.shape[0]
     line, wide = LINE, n_ex // LINE
@@ -33,7 +33,7 @@
     z, x = me // wide, lax.rem(me, wide)
     y, core = tp // CORES, lax.rem(tp, CORES)
     owner = me // per_owner
-    mine = owner == tp
+    mine = lax.rem(owner, CORES) == core
 
     def chunk(zz, xx, k):
         return (zz * wide + xx) * examples + k
@@ -64,22 +64,63 @@
     def _(ex):
         @pl.when(jnp.logical_not(jnp.logical_and(ex == me, mine)))
         def _():
-            greet(ex, owner)
+            greet(ex, y * CORES + lax.rem(owner, CORES))
 
     count = (z > 0).astype(jnp.int32) + (z < line - 1).astype(jnp.int32) - mine.astype(jnp.int32)
     pl.semaphore_wait(barrier, count + (wide - 1) + (ys - 1) + 1 + per_owner * n_tp)
 
-    def part(j, t):
-        return pltpu.make_async_remote_copy(
-            src_ref=act_ref.at[pl.ds(t * quarter, quarter), pl.ds(j * rows, rows)],
+    def to_relay(d, c):
+        to = other(y, d, ys)
+        return pltpu.make_async_remote_copy(
+            src_ref=act_ref.at[pl.ds((to * CORES + c) * quarter, quarter)], dst_ref=relay.at[y, c],
+            send_sem=relay_send.at[d * CORES + c], recv_sem=relay_recv.at[y * CORES + c],
+            device_id={"ex": me, "tp": to * CORES + core}, device_id_type=MESH)
+
+    def part(source, from_y, c, j):
+        t = y * CORES + c
+        return pltpu.make_async_remote_copy(
+            src_ref=source.at[:, pl.ds(j * rows, rows)],
             dst_ref=acts.at[me, pl.ds(t * quarter, quarter)],
-            send_sem=part_send.at[j * n_tp + t], recv_sem=part_recv.at[me],
-            device_id={"ex": tp * per_owner + j, "tp": t}, device_id_type=MESH)
-
-    def own_part(j):
+            send_sem=part_send.at[(from_y * CORES + c) * per_owner + j], recv_sem=part_recv.at[me],
+            device_id={"ex": (from_y * CORES + core) * per_owner + j, "tp": t}, device_id_type=MESH)
+
+    def own_part(source, j):
         return pltpu.make_async_copy(
-            act_ref.at[pl.ds(tp * quarter, quarter), pl.ds(j * rows, rows)],
+            source.at[:, pl.ds(j * rows, rows)],
             acts.at[me, pl.ds(tp * quarter, quarter)], part_recv.at[me])
+
+    def parts_from(source, from_y, c, begin):
+        for j in range(per_owner):
+            itself = jnp.logical_and((from_y * CORES + core) * per_owner + j == me, c == core)
+
+            @pl.when(jnp.logical_not(itself))
+            def _():
+                if begin:
+                    part(source, from_y, c, j).start()
+                else:
+                    part(source, from_y, c, j).wait_send()
+
+            if begin:
+                @pl.when(itself)
+                def _():
+                    own_part(source, j).start()
+
+    def direct_parts(begin):
+        for c in range(CORES):
+            parts_from(act_ref.at[pl.ds((y * CORES + c) * quarter, quarter)], y, c, begin)
+
+    def relayed_parts(begin):
+        for d in range(1, ys):
+            from_y = other(y, d, ys)
+            for c in range(CORES):
+                if begin:
+                    arrived(relay.at[from_y, c], relay_recv.at[from_y * CORES + c])
+                parts_from(relay.at[from_y, c], from_y, c, begin)
+
+    def relays(go):
+        for d in range(1, ys):
+            for c in range(CORES):
+                go(to_relay(d, c))
 
     def piece(ex, t):
         return acts.at[ex, pl.ds(t * quarter, quarter)]
@@ -117,29 +158,8 @@
     def own_load():
         return pltpu.make_async_copy(og_ref, ogs.at[pl.ds(me * examples, examples)], own_sem)
 
-    def each_part(act):
-        @pl.loop(0, per_owner * n_tp)
-        def _(i):
-            j, t = i // n_tp, lax.rem(i, n_tp)
-            itself = jnp.logical_and(tp * per_owner + j == me, t == tp)
-            act(j, t, itself)
-
-    def start_part(j, t, itself):
-        @pl.when(itself)
-        def _():
-            own_part(j).start()
-
-        @pl.when(jnp.logical_not(itself))
-        def _():
-            part(j, t).start()
-
-    def end_part(j, t, itself):
-        @pl.when(jnp.logical_not(itself))
-        def _():
-            part(j, t).wait_send()
-
-    def own_copies(go):
-        @pl.loop(0, examples)
+    def own_copies(go, first, last):
+        @pl.loop(first, last)
         def _(k):
             c = chunk(z, x, k)
             for d in range(1, wide):
@@ -201,32 +221,33 @@
     def nothing(c):
         pass
 
-    def act_source(i):
-        far = i // wide
-        below = jnp.minimum(z, line - 1 - z)
-        near = jnp.where(lax.rem(far, 2) == 1, z - (far + 1) // 2, z + far // 2)
-        end = jnp.where(z < line - 1 - z, far, line - 1 - far)
-        zz = jnp.where(far <= 2 * below, near, end)
-        return zz * wide + lax.rem(x + lax.rem(i, wide), wide)
-
-    def act_parts(first, last):
-        @pl.loop(first, last)
-        def _(i):
-            ex = act_source(i)
-            arrived(piece(ex, tp), part_recv.at[ex])
-            for d in range(1, ys):
-                share_y(ex, d).start()
-            share_core(ex, y).start()
-
-    def act_shares(first, last):
-        @pl.loop(first, last)
-        def _(i):
-            ex = act_source(i)
-            for d in range(1, ys):
-                yy = other(y, d, ys)
-                t = yy * CORES + core
-                arrived(piece(ex, t), share_recv.at[ex * n_tp + t])
-                share_core(ex, yy).start()
+    slots = wide + (line - 1) * 2 * wide
+
+    def at_slot(n, act):
+        far = n >= wide
+        m = jnp.maximum(n - wide, 0)
+        s = jnp.where(far, 1 + m // (2 * wide), 0)
+        d = jnp.where(far, lax.rem(m, 2 * wide) // 2, n)
+        zz = z + s * (2 * lax.rem(m, 2) - 1)
+
+        @pl.when(jnp.logical_and(jnp.logical_and(n >= 0, n < slots), jnp.logical_and(zz >= 0, zz < line)))
+        def _():
+            act(d, zz, lax.rem(x + d, wide))
+
+    def act_parts(d, zz, xx):
+        ex = zz * wide + xx
+        arrived(piece(ex, tp), part_recv.at[ex])
+        for e in range(1, ys):
+            share_y(ex, e).start()
+        share_core(ex, y).start()
+
+    def act_shares(d, zz, xx):
+        ex = zz * wide + xx
+        for e in range(1, ys):
+            yy = other(y, e, ys)
+            t = yy * CORES + core
+            arrived(piece(ex, t), share_recv.at[ex * n_tp + t])
+            share_core(ex, yy).start()
 
     col_tile = tile_of(width, 512)
 
@@ -239,38 +260,29 @@
             g = jnp.dot(lhs[...], ogs[ex * examples + k, :, q], preferred_element_type=jnp.float32)
             out_ref[:, q] += g * g
 
-    slots = wide + (line - 1) * 2 * wide
-
-    def add_source(n):
-        far = n >= wide
-        m = jnp.maximum(n - wide, 0)
-        s = jnp.where(far, 1 + m // (2 * wide), 0)
-        d = jnp.where(far, lax.rem(m, 2 * wide) // 2, n)
-        zz = z + s * (2 * lax.rem(m, 2) - 1)
-
-        @pl.when(jnp.logical_and(zz >= 0, zz < line))
-        def _():
-            xx = lax.rem(x + d, wide)
-            ex = zz * wide + xx
-            for yy in range(ys):
-                t = yy * CORES + 1 - core
-                arrived(piece(ex, t), share_recv.at[ex * n_tp + t])
-
-            @pl.loop(0, examples)
-            def _(k):
-                @pl.when(jnp.logical_and(d > 0, jnp.logical_or(zz != z, k >= BY_LINE)))
-                def _():
-                    og_ready(chunk(zz, xx, k))
-
-                add_example(ex, k)
-
-    each_part(start_part)
-    own_copies(start)
+    def add_source(d, zz, xx):
+        ex = zz * wide + xx
+        for yy in range(ys):
+            t = yy * CORES + 1 - core
+            arrived(piece(ex, t), share_recv.at[ex * n_tp + t])
+
+        @pl.loop(0, examples)
+        def _(k):
+            @pl.when(jnp.logical_and(d > 0, jnp.logical_or(zz != z, k >= BY_LINE)))
+            def _():
+                og_ready(chunk(zz, xx, k))
+
+            add_example(ex, k)
+
+    half = examples // 2
+    relays(start)
+    direct_parts(True)
+    own_copies(start, 0, half)
     own_load().start()
     out_ref[...] = jnp.zeros_like(out_ref)
+    relayed_parts(True)
+    own_copies(start, half, examples)
     own_load().wait()
-    each = -(-n_ex // examples)
-    more = -(-n_ex // (2 * examples))
 
     @pl.loop(0, examples + slots)
     def _(i):
@@ -280,26 +292,19 @@
         def _():
             line_step(start, og_ready, s, k)
 
-        @pl.when(s == 1)
-        def _():
-            act_parts(k * each, jnp.minimum(k * each + each, n_ex))
-
-        @pl.when(i == examples - 1)
+        @pl.when(i == 0)
         def _():
             side_copies(start, og_ready)
-            act_shares(0, more)
-
-        @pl.when(i >= examples)
-        def _():
-            @pl.when(s == 2)
-            def _():
-                first = more + k * each
-                act_shares(jnp.minimum(first, n_ex), jnp.minimum(first + each, n_ex))
-
-            add_source(i - examples)
-
-    each_part(end_part)
-    own_copies(sent)
+
+        n = i - examples
+        at_slot(n + 2, act_parts)
+        at_slot(n + 1, act_shares)
+        at_slot(n, add_source)
+
+    relays(sent)
+    direct_parts(False)
+    relayed_parts(False)
+    own_copies(sent, 0, examples)
 
     @pl.loop(0, (line - 1) * examples)
     def _(i):
@@ -329,11 +334,12 @@
         return pl.pallas_call(
             functools.partial(kernel, n_ex, n_tp),
             out_shape=jax.ShapeDtypeStruct((rows, width), jnp.float32),
-            in_specs=[pl.BlockSpec(memory_space=pl.ANY)] * 2,
+            in_specs=[pl.BlockSpec(memory_space=pltpu.HBM)] * 2,
             out_specs=pl.BlockSpec(memory_space=pltpu.VMEM),
             scratch_shapes=[
                 pltpu.VMEM((n_ex, examples * tokens, rows), jnp.bfloat16),
                 pltpu.VMEM((chunks, tokens, width), jnp.bfloat16),
+                pltpu.VMEM((ys, CORES, examples * tokens // n_tp, width), jnp.bfloat16),
                 pltpu.VMEM((rows, tokens), jnp.bfloat16),
                 dma,
                 dma((chunks,)),
@@ -342,6 +348,8 @@
                 dma((chunks * wide,)),
                 dma((width // rows * n_tp,)),
                 dma((n_ex,)),
+                dma((n_tp,)),
+                dma((n_tp,)),
                 dma((n_ex * ys,)),
                 dma((n_ex * ys,)),
                 dma((n_ex * n_tp,)),

time: 260 us -> 229 us (0.88)
  Pallas kernels: 253 us -> 222 us
    pallas_call x1, Pallas kernels: 253 us -> 222 us  [body(): pl.pallas_call(functools.partial(kernel, n_ex, n_tp), out_shape=jax.Shape...]
where the time goes in v3:
time: 229 us; the launch traced here: 228 us
  Pallas kernels  222 us (97%)
  local copies, waits for them, and re-layouts  6.58 us (3%)
    pallas_call x1, Pallas kernels, body(): pl.pallas_call(functools.partial(kernel, n_ex, n_tp), out_shape=jax.Shape...  222 us
    unnamed x5, local copies, waits for them, and re-layouts  6.58 us

profile of v3, /device:TPU:0, one launch (start us, length us, event | category | flops | bytes accessed | tf_op | source)
XLA Modules:
  0.0 228.2 jit_solution(286208915535108864)
XLA Ops:
  0.0 0.0 copy-start
  0.0 1.6 copy-done
  1.6 0.0 copy-start.1
  1.6 1.6 copy-done.1
  3.2 221.6 %shard_map.28 = f32[1024,2048]{1,0:T(8,128)S(1)} custom-call(bf16[512,2048]{1,0:T(8,128)(2,1)S(1)} %bitcast.1, bf16[4,128,2048]{2,1,0:T(8,128)(2,1)S(1)} %copy-done.1), custom_call_target="tpu_custom_call" | custom-call | flops 17179869184 | bytes 12582912 | tf_op jit(solution)/shard_map/pallas_call | solution.py:334
  224.8 3.4 %copy.4 = f32[1024,2048]{1,0:T(8,128)} copy(f32[1024,2048]{1,0:T(8,128)S(1)} %shard_map.28) | data formatting | bytes 16777216
Async XLA Ops:
  0.0 1.6 copy-start
  1.6 1.6 copy-start.1

commit v4 on v3

--- a/solution.py
+++ b/solution.py
@@ -195,11 +195,15 @@
                     for d in range(1, wide):
                         go(across(c, ogs.at[c], d))
 
-    def side_copies(go, ready):
+    def side_ready():
+        for k in range(BY_LINE):
+            for d in range(1, wide):
+                og_ready(chunk(z, other(x, d, wide), k))
+
+    def side_copies(go):
         for k in range(BY_LINE):
             for d in range(1, wide):
                 c = chunk(z, other(x, d, wide), k)
-                ready(c)
 
                 @pl.when(z < line - 1)
                 def _():
@@ -221,16 +225,15 @@
     def nothing(c):
         pass
 
-    slots = wide + (line - 1) * 2 * wide
-
     def at_slot(n, act):
-        far = n >= wide
-        m = jnp.maximum(n - wide, 0)
-        s = jnp.where(far, 1 + m // (2 * wide), 0)
-        d = jnp.where(far, lax.rem(m, 2 * wide) // 2, n)
-        zz = z + s * (2 * lax.rem(m, 2) - 1)
-
-        @pl.when(jnp.logical_and(jnp.logical_and(n >= 0, n < slots), jnp.logical_and(zz >= 0, zz < line)))
+        far = n // wide
+        below = jnp.minimum(z, line - 1 - z)
+        near = jnp.where(lax.rem(far, 2) == 1, z - (far + 1) // 2, z + far // 2)
+        end = jnp.where(z < line - 1 - z, far, line - 1 - far)
+        zz = jnp.where(far <= 2 * below, near, end)
+        d = lax.rem(n, wide)
+
+        @pl.when(jnp.logical_and(n >= 0, n < n_ex))
         def _():
             act(d, zz, lax.rem(x + d, wide))
 
@@ -268,11 +271,28 @@
 
         @pl.loop(0, examples)
         def _(k):
-            @pl.when(jnp.logical_and(d > 0, jnp.logical_or(zz != z, k >= BY_LINE)))
+            by_line = jnp.logical_and(jnp.logical_or(zz == z - 1, zz == z + 1), k < BY_LINE)
+            across_here = jnp.logical_or(zz != z, k >= BY_LINE)
+
+            @pl.when(jnp.logical_and(jnp.logical_and(d > 0, across_here), jnp.logical_not(by_line)))
             def _():
                 og_ready(chunk(zz, xx, k))
 
-            add_example(ex, k)
+            @pl.when(jnp.logical_not(jnp.logical_and(d > 0, by_line)))
+            def _():
+                add_example(ex, k)
+
+    def add_by_line():
+        for step in (-1, 1):
+            zz = z + step
+
+            @pl.when(jnp.logical_and(zz >= 0, zz < line))
+            def _():
+                @pl.loop(0, (wide - 1) * BY_LINE)
+                def _(i):
+                    xx, k = lax.rem(x + 1 + i // BY_LINE, wide), lax.rem(i, BY_LINE)
+                    og_ready(chunk(zz, xx, k))
+                    add_example(zz * wide + xx, k)
 
     half = examples // 2
     relays(start)
@@ -284,7 +304,9 @@
     own_copies(start, half, examples)
     own_load().wait()
 
-    @pl.loop(0, examples + slots)
+    last = n_ex - wide
+
+    @pl.loop(0, examples + n_ex + 1)
     def _(i):
         s, k = 1 + i // examples, lax.rem(i, examples)
 
@@ -292,14 +314,21 @@
         def _():
             line_step(start, og_ready, s, k)
 
-        @pl.when(i == 0)
-        def _():
-            side_copies(start, og_ready)
+        @pl.when(i == examples - 1)
+        def _():
+            side_ready()
+
+        @pl.when(i == (line - 2) * examples)
+        def _():
+            side_copies(start)
 
         n = i - examples
         at_slot(n + 2, act_parts)
         at_slot(n + 1, act_shares)
-        at_slot(n, add_source)
+
+        at_slot(jnp.where(n < last, n, jnp.where(n == last, -1, n - 1)), add_source)
+
+    add_by_line()
 
     relays(sent)
     direct_parts(False)
@@ -310,7 +339,7 @@
     def _(i):
         line_step(sent, nothing, 1 + i // examples, lax.rem(i, examples))
 
-    side_copies(sent, nothing)
+    side_copies(sent)
 
     @pl.loop(0, n_ex)
     def _(ex):

time: 229 us -> 211 us (0.921)
  Pallas kernels: 222 us -> 204 us
    pallas_call x1, Pallas kernels: 222 us -> 204 us  [body(): pl.pallas_call(functools.partial(kernel, n_ex, n_tp), out_shape=jax.Shape...]
where the time goes in v4:
time: 211 us
  Pallas kernels  204 us (97%)
  local copies, waits for them, and re-layouts  6.58 us (3%)
    pallas_call x1, Pallas kernels, body(): pl.pallas_call(functools.partial(kernel, n_ex, n_tp), out_shape=jax.Shape...  204 us
    unnamed x5, local copies, waits for them, and re-layouts  6.58 us

profile of v4, /device:TPU:0, one launch (start us, length us, event | category | flops | bytes accessed | tf_op | source)
XLA Modules:
  0.0 211.0 jit_solution(13044943001617888407)
XLA Ops:
  0.0 0.0 copy-start
  0.0 1.6 copy-done
  1.6 0.0 copy-start.1
  1.6 1.6 copy-done.1
  3.2 204.5 %shard_map.28 = f32[1024,2048]{1,0:T(8,128)S(1)} custom-call(bf16[512,2048]{1,0:T(8,128)(2,1)S(1)} %bitcast.1, bf16[4,128,2048]{2,1,0:T(8,128)(2,1)S(1)} %copy-done.1), custom_call_target="tpu_custom_call" | custom-call | flops 17179869184 | bytes 12582912 | tf_op jit(solution)/shard_map/pallas_call | solution.py:363
  207.6 3.4 %copy.4 = f32[1024,2048]{1,0:T(8,128)} copy(f32[1024,2048]{1,0:T(8,128)S(1)} %shard_map.28) | data formatting | bytes 16777216
Async XLA Ops:
  0.0 1.6 copy-start
  1.6 1.6 copy-start.1

commit v5 on v4

--- a/solution.py
+++ b/solution.py
@@ -9,7 +9,8 @@
 
 MESH = pl.DeviceIdType.MESH
 LINE = 4
-BY_LINE = 1
+SPLIT = 2
+BY_LINE = 3
 CORES = 2
 
 
@@ -24,6 +25,7 @@
            part_send, part_recv, relay_send, relay_recv, y_send, sib_send, share_recv):
     examples, tokens, width = og_ref.shape
     rows = out_ref.shape[0]
+    pieces, cut = examples * SPLIT, width // SPLIT
     line, wide = LINE, n_ex // LINE
     per_owner = width // rows
     ys = n_tp // CORES
@@ -36,7 +38,7 @@
     mine = lax.rem(owner, CORES) == core
 
     def chunk(zz, xx, k):
-        return (zz * wide + xx) * examples + k
+        return (zz * wide + xx) * pieces + k
 
     def other(first, step, size):
         return lax.rem(first + step, size)
@@ -155,23 +157,26 @@
     def across(c, source, d):
         return og_copy(c, source, across_send, c * wide + d, z * wide + other(x, d, wide))
 
-    def own_load():
-        return pltpu.make_async_copy(og_ref, ogs.at[pl.ds(me * examples, examples)], own_sem)
+    def own_load(h):
+        return pltpu.make_async_copy(
+            og_ref.at[:, :, pl.ds(h * cut, cut)],
+            ogs.at[pl.ds(me * pieces + h * examples, examples)], own_sem.at[h])
 
     def own_copies(go, first, last):
         @pl.loop(first, last)
         def _(k):
             c = chunk(z, x, k)
+            own = og_ref.at[lax.rem(k, examples), :, pl.ds(pl.multiple_of(k // examples * cut, cut), cut)]
             for d in range(1, wide):
-                go(across(c, og_ref.at[k], d))
+                go(across(c, own, d))
 
             @pl.when(z < line - 1)
             def _():
-                go(up(c, og_ref.at[k]))
+                go(up(c, own))
 
             @pl.when(z > 0)
             def _():
-                go(down(c, og_ref.at[k]))
+                go(down(c, own))
 
     def line_step(go, ready, s, k):
         for step in (-1, 1):
@@ -252,16 +257,18 @@
             arrived(piece(ex, t), share_recv.at[ex * n_tp + t])
             share_core(ex, yy).start()
 
-    col_tile = tile_of(width, 512)
-
-    def add_example(ex, k):
+    col_tile = tile_of(cut, 512)
+
+    def add_piece(ex, u):
+        k, h = lax.rem(u, examples), u // examples
         lhs[...] = acts[ex, pl.ds(pl.multiple_of(k * tokens, tokens), tokens), :].T
 
-        @pl.loop(0, width // col_tile)
+        @pl.loop(0, cut // col_tile)
         def _(j):
             q = pl.ds(pl.multiple_of(j * col_tile, col_tile), col_tile)
-            g = jnp.dot(lhs[...], ogs[ex * examples + k, :, q], preferred_element_type=jnp.float32)
-            out_ref[:, q] += g * g
+            to = pl.ds(pl.multiple_of(h * cut + j * col_tile, col_tile), col_tile)
+            g = jnp.dot(lhs[...], ogs[ex * pieces + u, :, q], preferred_element_type=jnp.float32)
+            out_ref[:, to] += g * g
 
     def add_source(d, zz, xx):
         ex = zz * wide + xx
@@ -269,7 +276,7 @@
             t = yy * CORES + 1 - core
             arrived(piece(ex, t), share_recv.at[ex * n_tp + t])
 
-        @pl.loop(0, examples)
+        @pl.loop(0, pieces)
         def _(k):
             by_line = jnp.logical_and(jnp.logical_or(zz == z - 1, zz == z + 1), k < BY_LINE)
             across_here = jnp.logical_or(zz != z, k >= BY_LINE)
@@ -280,7 +287,7 @@
 
             @pl.when(jnp.logical_not(jnp.logical_and(d > 0, by_line)))
             def _():
-                add_example(ex, k)
+                add_piece(ex, k)
 
     def add_by_line():
         for step in (-1, 1):
@@ -292,52 +299,56 @@
                 def _(i):
                     xx, k = lax.rem(x + 1 + i // BY_LINE, wide), lax.rem(i, BY_LINE)
                     og_ready(chunk(zz, xx, k))
-                    add_example(zz * wide + xx, k)
-
-    half = examples // 2
+                    add_piece(zz * wide + xx, k)
+
+    half = pieces // 2
     relays(start)
     direct_parts(True)
     own_copies(start, 0, half)
-    own_load().start()
+    for h in range(SPLIT):
+        own_load(h).start()
     out_ref[...] = jnp.zeros_like(out_ref)
     relayed_parts(True)
-    own_copies(start, half, examples)
-    own_load().wait()
+    own_copies(start, half, pieces)
+    for h in range(SPLIT):
+        own_load(h).wait()
 
     last = n_ex - wide
 
-    @pl.loop(0, examples + n_ex + 1)
+    @pl.loop(0, SPLIT * (examples + n_ex + 1))
     def _(i):
-        s, k = 1 + i // examples, lax.rem(i, examples)
+        s, k = 1 + i // pieces, lax.rem(i, pieces)
 
         @pl.when(s < line)
         def _():
             line_step(start, og_ready, s, k)
 
-        @pl.when(i == examples - 1)
+        @pl.when(i == pieces - 1)
         def _():
             side_ready()
 
-        @pl.when(i == (line - 2) * examples)
+        @pl.when(i == (line - 2) * pieces)
         def _():
             side_copies(start)
 
-        n = i - examples
-        at_slot(n + 2, act_parts)
-        at_slot(n + 1, act_shares)
-
-        at_slot(jnp.where(n < last, n, jnp.where(n == last, -1, n - 1)), add_source)
+        @pl.when(lax.rem(i, SPLIT) == SPLIT - 1)
+        def _():
+            n = i // SPLIT - examples
+            at_slot(n + 2, act_parts)
+            at_slot(n + 1, act_shares)
+
+            at_slot(jnp.where(n < last, n, jnp.where(n == last, -1, n - 1)), add_source)
 
     add_by_line()
 
     relays(sent)
     direct_parts(False)
     relayed_parts(False)
-    own_copies(sent, 0, examples)
-
-    @pl.loop(0, (line - 1) * examples)
+    own_copies(sent, 0, pieces)
+
+    @pl.loop(0, (line - 1) * pieces)
     def _(i):
-        line_step(sent, nothing, 1 + i // examples, lax.rem(i, examples))
+        line_step(sent, nothing, 1 + i // pieces, lax.rem(i, pieces))
 
     side_copies(sent)
 
@@ -356,7 +367,7 @@
         examples, tokens, width = out_grads.shape
         rows = width * n_tp // n_ex
         flat = activations.reshape(examples * tokens, width)
-        chunks = n_ex * examples
+        chunks = n_ex * examples * SPLIT
         wide = n_ex // LINE
         ys = n_tp // CORES
         dma = pltpu.SemaphoreType.DMA
@@ -367,10 +378,10 @@
             out_specs=pl.BlockSpec(memory_space=pltpu.VMEM),
             scratch_shapes=[
                 pltpu.VMEM((n_ex, examples * tokens, rows), jnp.bfloat16),
-                pltpu.VMEM((chunks, tokens, width), jnp.bfloat16),
+                pltpu.VMEM((chunks, tokens, width // SPLIT), jnp.bfloat16),
                 pltpu.VMEM((ys, CORES, examples * tokens // n_tp, width), jnp.bfloat16),
                 pltpu.VMEM((rows, tokens), jnp.bfloat16),
-                dma,
+                dma((SPLIT,)),
                 dma((chunks,)),
                 dma((chunks,)),
                 dma((chunks,)),
@@ -386,9 +397,12 @@
             compiler_params=pltpu.CompilerParams(
                 collective_id=0, has_side_effects=True, vmem_limit_bytes=40 * 1024 * 1024),
             cost_estimate=pl.CostEstimate(
-                flops=2 * rows * width * chunks * tokens,
+                flops=2 * rows * width * n_ex * examples * tokens,
                 bytes_accessed=12 * 1024 * 1024, transcendentals=0),
-        )(flat, out_grads)
+        )(
+            pltpu.with_memory_space_constraint(flat, pltpu.HBM),
+            pltpu.with_memory_space_constraint(out_grads, pltpu.HBM),
+        )
 
     return jax.shard_map(
         body,

time: 211 us -> 211 us (level)
  Pallas kernels: 204 us -> 208 us
  local copies, waits for them, and re-layouts: 6.58 us -> 3.4 us
    pallas_call x1, Pallas kernels: 204 us -> 208 us  [body(): pl.pallas_call(functools.partial(kernel, n_ex, n_tp), out_shape=jax.Shape...]
    unnamed x5 -> x1, local copies, waits for them, and re-layouts: 6.58 us -> 3.4 us
where the time goes in v5:
time: 211 us
  Pallas kernels  208 us (99%)
  local copies, waits for them, and re-layouts  3.4 us (2%)
    pallas_call x1, Pallas kernels, body(): pl.pallas_call(functools.partial(kernel, n_ex, n_tp), out_shape=jax.Shape...  208 us

profile of v5, /device:TPU:0, one launch (start us, length us, event | category | flops | bytes accessed | tf_op | source)
XLA Modules:
  0.0 211.3 jit_solution(14330780966691600521)
XLA Ops:
  0.0 207.9 %shard_map.28 = f32[1024,2048]{1,0:T(8,128)S(1)} custom-call(bf16[512,2048]{1,0:T(8,128)(2,1)} %bitcast.1, bf16[4,128,2048]{2,1,0:T(8,128)(2,1)} %og_ref.1), custom_call_target="tpu_custom_call" | custom-call | flops 17179869184 | bytes 12582912 | tf_op jit(solution)/shard_map/pallas_call | solution.py:374
  207.9 3.4 %copy.4 = f32[1024,2048]{1,0:T(8,128)} copy(f32[1024,2048]{1,0:T(8,128)S(1)} %shard_map.28) | data formatting | bytes 16777216

commit v6 on v5

--- a/solution.py
+++ b/solution.py
@@ -34,8 +34,6 @@
     me, tp = lax.axis_index("ex"), lax.axis_index("tp")
     z, x = me // wide, lax.rem(me, wide)
     y, core = tp // CORES, lax.rem(tp, CORES)
-    owner = me // per_owner
-    mine = lax.rem(owner, CORES) == core
 
     def chunk(zz, xx, k):
         return (zz * wide + xx) * pieces + k
@@ -48,81 +46,63 @@
     def greet(ex, t):
         pl.semaphore_signal(barrier, inc=1, device_id={"ex": ex, "tp": t}, device_id_type=MESH)
 
-    @pl.when(z > 0)
-    def _():
-        greet(me - wide, tp)
-
-    @pl.when(z < line - 1)
-    def _():
-        greet(me + wide, tp)
-
-    for d in range(1, wide):
-        greet(z * wide + other(x, d, wide), tp)
-    for d in range(1, ys):
-        greet(me, other(y, d, ys) * CORES + core)
-    greet(me, y * CORES + 1 - core)
-
-    @pl.loop(0, n_ex)
-    def _(ex):
-        @pl.when(jnp.logical_not(jnp.logical_and(ex == me, mine)))
-        def _():
-            greet(ex, y * CORES + lax.rem(owner, CORES))
-
-    count = (z > 0).astype(jnp.int32) + (z < line - 1).astype(jnp.int32) - mine.astype(jnp.int32)
-    pl.semaphore_wait(barrier, count + (wide - 1) + (ys - 1) + 1 + per_owner * n_tp)
-
-    def to_relay(d, c):
-        to = other(y, d, ys)
+    for d in range(1, n_ex):
+        greet(other(me, d, n_ex), tp)
+    for d in range(1, n_tp):
+        greet(me, other(tp, d, n_tp))
+    pl.semaphore_wait(barrier, n_ex - 1 + n_tp - 1)
+
+    def others():
+        for dy in range(ys):
+            for dc in range(CORES):
+                if dy + dc:
+                    yield dy * CORES + dc, other(y, dy, ys) * CORES + other(core, dc, CORES)
+
+    def to_relay(slot, t):
         return pltpu.make_async_remote_copy(
-            src_ref=act_ref.at[pl.ds((to * CORES + c) * quarter, quarter)], dst_ref=relay.at[y, c],
-            send_sem=relay_send.at[d * CORES + c], recv_sem=relay_recv.at[y * CORES + c],
-            device_id={"ex": me, "tp": to * CORES + core}, device_id_type=MESH)
-
-    def part(source, from_y, c, j):
-        t = y * CORES + c
+            src_ref=act_ref.at[pl.ds(t * quarter, quarter)], dst_ref=relay.at[tp],
+            send_sem=relay_send.at[slot], recv_sem=relay_recv.at[tp],
+            device_id={"ex": me, "tp": t}, device_id_type=MESH)
+
+    def part(source, ex, j):
         return pltpu.make_async_remote_copy(
-            src_ref=source.at[:, pl.ds(j * rows, rows)],
-            dst_ref=acts.at[me, pl.ds(t * quarter, quarter)],
-            send_sem=part_send.at[(from_y * CORES + c) * per_owner + j], recv_sem=part_recv.at[me],
-            device_id={"ex": (from_y * CORES + core) * per_owner + j, "tp": t}, device_id_type=MESH)
+            src_ref=source.at[:, pl.ds(j * rows, rows)], dst_ref=acts.at[me, pl.ds(tp * quarter, quarter)],
+            send_sem=part_send.at[ex], recv_sem=part_recv.at[me],
+            device_id={"ex": ex, "tp": tp}, device_id_type=MESH)
 
     def own_part(source, j):
         return pltpu.make_async_copy(
             source.at[:, pl.ds(j * rows, rows)],
             acts.at[me, pl.ds(tp * quarter, quarter)], part_recv.at[me])
 
-    def parts_from(source, from_y, c, begin):
+    def parts_from(source, t, begin):
         for j in range(per_owner):
-            itself = jnp.logical_and((from_y * CORES + core) * per_owner + j == me, c == core)
-
-            @pl.when(jnp.logical_not(itself))
+            ex = t * per_owner + j
+
+            @pl.when(ex != me)
             def _():
                 if begin:
-                    part(source, from_y, c, j).start()
+                    part(source, ex, j).start()
                 else:
-                    part(source, from_y, c, j).wait_send()
+                    part(source, ex, j).wait_send()
 
             if begin:
-                @pl.when(itself)
+                @pl.when(ex == me)
                 def _():
                     own_part(source, j).start()
 
     def direct_parts(begin):
-        for c in range(CORES):
-            parts_from(act_ref.at[pl.ds((y * CORES + c) * quarter, quarter)], y, c, begin)
+        parts_from(act_ref.at[pl.ds(tp * quarter, quarter)], tp, begin)
 
     def relayed_parts(begin):
-        for d in range(1, ys):
-            from_y = other(y, d, ys)
-            for c in range(CORES):
-                if begin:
-                    arrived(relay.at[from_y, c], relay_recv.at[from_y * CORES + c])
-                parts_from(relay.at[from_y, c], from_y, c, begin)
+        for slot, t in others():
+            if begin:
+                arrived(relay.at[t], relay_recv.at[t])
+            parts_from(relay.at[t], t, begin)
 
     def relays(go):
-        for d in range(1, ys):
-            for c in range(CORES):
-                go(to_relay(d, c))
+        for slot, t in others():
+            go(to_relay(slot, t))
 
     def piece(ex, t):
         return acts.at[ex, pl.ds(t * quarter, quarter)]
@@ -257,18 +237,26 @@
             arrived(piece(ex, t), share_recv.at[ex * n_tp + t])
             share_core(ex, yy).start()
 
-    col_tile = tile_of(cut, 512)
+    row_tile, col_tile = tile_of(rows, 256), tile_of(cut, 256)
+    body = 2 * col_tile if cut % (2 * col_tile) == 0 else col_tile
+
+    def turn(ex, k):
+        lhs[k] = acts[ex, pl.ds(pl.multiple_of(k * tokens, tokens), tokens), :].T
 
     def add_piece(ex, u):
         k, h = lax.rem(u, examples), u // examples
-        lhs[...] = acts[ex, pl.ds(pl.multiple_of(k * tokens, tokens), tokens), :].T
-
-        @pl.loop(0, cut // col_tile)
-        def _(j):
-            q = pl.ds(pl.multiple_of(j * col_tile, col_tile), col_tile)
-            to = pl.ds(pl.multiple_of(h * cut + j * col_tile, col_tile), col_tile)
-            g = jnp.dot(lhs[...], ogs[ex * pieces + u, :, q], preferred_element_type=jnp.float32)
-            out_ref[:, to] += g * g
+
+        @pl.loop(0, cut // body)
+        def _(i):
+            for j in range(body // col_tile):
+                start_at = i * body + j * col_tile
+                q = pl.ds(pl.multiple_of(start_at, col_tile), col_tile)
+                to = pl.ds(pl.multiple_of(h * cut + start_at, col_tile), col_tile)
+                right = ogs[ex * pieces + u, :, q]
+                for m in range(rows // row_tile):
+                    r = pl.ds(m * row_tile, row_tile)
+                    g = jnp.dot(lhs[k, r, :], right, preferred_element_type=jnp.float32)
+                    out_ref[r, to] += g * g
 
     def add_source(d, zz, xx):
         ex = zz * wide + xx
@@ -276,6 +264,10 @@
             t = yy * CORES + 1 - core
             arrived(piece(ex, t), share_recv.at[ex * n_tp + t])
 
+        @pl.loop(0, examples)
+        def _(k):
+            turn(ex, k)
+
         @pl.loop(0, pieces)
         def _(k):
             by_line = jnp.logical_and(jnp.logical_or(zz == z - 1, zz == z + 1), k < BY_LINE)
@@ -299,6 +291,7 @@
                 def _(i):
                     xx, k = lax.rem(x + 1 + i // BY_LINE, wide), lax.rem(i, BY_LINE)
                     og_ready(chunk(zz, xx, k))
+                    turn(zz * wide + xx, lax.rem(k, examples))
                     add_piece(zz * wide + xx, k)
 
     half = pieces // 2
@@ -379,14 +372,14 @@
             scratch_shapes=[
                 pltpu.VMEM((n_ex, examples * tokens, rows), jnp.bfloat16),
                 pltpu.VMEM((chunks, tokens, width // SPLIT), jnp.bfloat16),
-                pltpu.VMEM((ys, CORES, examples * tokens // n_tp, width), jnp.bfloat16),
-                pltpu.VMEM((rows, tokens), jnp.bfloat16),
+                pltpu.VMEM((n_tp, examples * tokens // n_tp, width), jnp.bfloat16),
+                pltpu.VMEM((examples, rows, tokens), jnp.bfloat16),
                 dma((SPLIT,)),
                 dma((chunks,)),
                 dma((chunks,)),
                 dma((chunks,)),
                 dma((chunks * wide,)),
-                dma((width // rows * n_tp,)),
+                dma((n_ex,)),
                 dma((n_ex,)),
                 dma((n_tp,)),
                 dma((n_tp,)),

time: 211 us -> 205 us (0.972)
  Pallas kernels: 208 us -> 201 us
    pallas_call x1, Pallas kernels: 208 us -> 201 us  [body(): pl.pallas_call(functools.partial(kernel, n_ex, n_tp), out_shape=jax.Shape...]
where the time goes in v6:
time: 205 us; the launch traced here: 204 us
  Pallas kernels  201 us (98%)
  local copies, waits for them, and re-layouts  3.4 us (2%)
    pallas_call x1, Pallas kernels, body(): pl.pallas_call(functools.partial(kernel, n_ex, n_tp), out_shape=jax.Shape...  201 us

profile of v6, /device:TPU:0, one launch (start us, length us, event | category | flops | bytes accessed | tf_op | source)
XLA Modules:
  0.0 204.5 jit_solution(3254420928165383720)
XLA Ops:
  0.0 201.1 %shard_map.28 = f32[1024,2048]{1,0:T(8,128)S(1)} custom-call(bf16[512,2048]{1,0:T(8,128)(2,1)} %bitcast.1, bf16[4,128,2048]{2,1,0:T(8,128)(2,1)} %og_ref.1), custom_call_target="tpu_custom_call" | custom-call | flops 17179869184 | bytes 12582912 | tf_op jit(solution)/shard_map/pallas_call | solution.py:367
  201.1 3.4 %copy.4 = f32[1024,2048]{1,0:T(8,128)} copy(f32[1024,2048]{1,0:T(8,128)S(1)} %shard_map.28) | data formatting | bytes 16777216

commit v7 on v6

--- a/solution.py
+++ b/solution.py
@@ -10,7 +10,7 @@
 MESH = pl.DeviceIdType.MESH
 LINE = 4
 SPLIT = 2
-BY_LINE = 3
+BY_LINE = 2
 CORES = 2
 
 
@@ -330,9 +330,11 @@
             at_slot(n + 2, act_parts)
             at_slot(n + 1, act_shares)
 
+            @pl.when(n == n_ex)
+            def _():
+                add_by_line()
+
             at_slot(jnp.where(n < last, n, jnp.where(n == last, -1, n - 1)), add_source)
-
-    add_by_line()
 
     relays(sent)
     direct_parts(False)

time: 205 us -> 207 us (level)
  Pallas kernels: 201 us -> 204 us
    pallas_call x1, Pallas kernels: 201 us -> 204 us  [body(): pl.pallas_call(functools.partial(kernel, n_ex, n_tp), out_shape=jax.Shape...]
where the time goes in v7:
time: 207 us
  Pallas kernels  204 us (99%)
  local copies, waits for them, and re-layouts  3.4 us (2%)
    pallas_call x1, Pallas kernels, body(): pl.pallas_call(functools.partial(kernel, n_ex, n_tp), out_shape=jax.Shape...  204 us

profile of v7, /device:TPU:0, one launch (start us, length us, event | category | flops | bytes accessed | tf_op | source)
XLA Modules:
  0.0 207.0 jit_solution(16168033519870115149)
XLA Ops:
  0.0 203.6 %shard_map.28 = f32[1024,2048]{1,0:T(8,128)S(1)} custom-call(bf16[512,2048]{1,0:T(8,128)(2,1)} %bitcast.1, bf16[4,128,2048]{2,1,0:T(8,128)(2,1)} %og_ref.1), custom_call_target="tpu_custom_call" | custom-call | flops 17179869184 | bytes 12582912 | tf_op jit(solution)/shard_map/pallas_call | solution.py:369
  203.6 3.4 %copy.4 = f32[1024,2048]{1,0:T(8,128)} copy(f32[1024,2048]{1,0:T(8,128)S(1)} %shard_map.28) | data formatting | bytes 16777216

commit v8 on v6

--- a/solution.py
+++ b/solution.py
@@ -287,12 +287,18 @@
 
             @pl.when(jnp.logical_and(zz >= 0, zz < line))
             def _():
-                @pl.loop(0, (wide - 1) * BY_LINE)
-                def _(i):
-                    xx, k = lax.rem(x + 1 + i // BY_LINE, wide), lax.rem(i, BY_LINE)
-                    og_ready(chunk(zz, xx, k))
-                    turn(zz * wide + xx, lax.rem(k, examples))
-                    add_piece(zz * wide + xx, k)
+                @pl.loop(1, wide)
+                def _(d):
+                    xx = lax.rem(x + d, wide)
+
+                    @pl.loop(0, min(BY_LINE, examples))
+                    def _(k):
+                        turn(zz * wide + xx, k)
+
+                    @pl.loop(0, BY_LINE)
+                    def _(k):
+                        og_ready(chunk(zz, xx, k))
+                        add_piece(zz * wide + xx, k)
 
     half = pieces // 2
     relays(start)

time: 205 us -> 205 us (level)
  no operation moved by 1% of the time
where the time goes in v8:
time: 205 us; the launch traced here: 204 us
  Pallas kernels  201 us (98%)
  local copies, waits for them, and re-layouts  3.4 us (2%)
    pallas_call x1, Pallas kernels, body(): pl.pallas_call(functools.partial(kernel, n_ex, n_tp), out_shape=jax.Shape...  201 us

profile of v8, /device:TPU:0, one launch (start us, length us, event | category | flops | bytes accessed | tf_op | source)
XLA Modules:
  0.0 204.4 jit_solution(14228383465796783623)
XLA Ops:
  0.0 201.0 %shard_map.28 = f32[1024,2048]{1,0:T(8,128)S(1)} custom-call(bf16[512,2048]{1,0:T(8,128)(2,1)} %bitcast.1, bf16[4,128,2048]{2,1,0:T(8,128)(2,1)} %og_ref.1), custom_call_target="tpu_custom_call" | custom-call | flops 17179869184 | bytes 12582912 | tf_op jit(solution)/shard_map/pallas_call | solution.py:373
  201.0 3.4 %copy.4 = f32[1024,2048]{1,0:T(8,128)} copy(f32[1024,2048]{1,0:T(8,128)S(1)} %shard_map.28) | data formatting | bytes 16777216
